TPU v7x, 32 devices: a whole 2x2x4 slice. The times are simulated.
32 devices in a mesh: ty: 8 (over z, x), tx: 4 (over y, core).
Axes of the slice: x: 2, y: 2, z: 4, core: 2. Of those that a mesh axis runs over, the one named last changes fastest.
Arguments:
- fixed_image: float32 [512, 1024], P('ty', 'tx'), may hold values from -6 to 6
- moving_image: float32 [512, 1024], P('ty', 'tx'), may hold values from -6 to 6
- tissue: int32 [16, 32], P('ty', 'tx'), may hold values from 0 to 1, as said below
Outputs:
- coefficients: float32 [2, 16, 32], P(None, 'ty', 'tx')
- mismatch: float32 [512, 1024], P('ty', 'tx')
Inputs may be any that keep to these rules, and one draw needn't show every extreme that they name: 1 marks a block of 32 x 32 fine pixels that holds tissue, 0 background.
All inputs are finite; a program needn't handle non-finite values.
Results may differ from a plain program's by a relative error of at most 0.0003.
Values sent between devices are 32-bit elements; how exact they have to be, the bound alone decides.
A program may use at most 64 MiB of HBM per device.

v0:
```python
import jax
import jax.numpy as jnp
from jax import lax
from jax.sharding import PartitionSpec as P

SPACE = 32
HALO = 6
MB = 32
ITERS = 2


offset_pairs = (
    (0, 2),
    (0, -2),
    (2, 0),
    (-2, 0),
    (2, 2),
    (2, -2),
    (-2, 2),
    (-2, -2),
    (0, 4),
    (0, -4),
    (4, 0),
    (-4, 0),
)
highest = lax.Precision.HIGHEST


def with_halo(block, sides, width):
    for axis, dim in sides:
        count = lax.axis_size(axis)
        forward = [(i, i + 1) for i in range(count - 1)]
        backward = [(target, source) for source, target in forward]
        low = lax.ppermute(
            lax.slice_in_dim(block, block.shape[dim] - width, None, axis=dim), axis, forward
        )
        high = lax.ppermute(lax.slice_in_dim(block, 0, width, axis=dim), axis, backward)
        block = jnp.concatenate([low, block, high], axis=dim)
    return block


def bspline(values):
    magnitude = jnp.abs(values)
    near_part = 2.0 / 3.0 - magnitude * magnitude + 0.5 * magnitude**3
    far_part = (2.0 - magnitude) ** 3 / 6.0
    return jnp.where(
        magnitude < 1.0, near_part, jnp.where(magnitude < 2.0, far_part, 0.0 * magnitude)
    )


def box_mean(values):
    height, breadth = values.shape
    total = values[0 : height - 2, 0 : breadth - 2]
    for shift_y in range(3):
        for shift_x in range(3):
            if shift_y + shift_x > 0:
                total = (
                    total + values[shift_y : height - 2 + shift_y, shift_x : breadth - 2 + shift_x]
                )
    return total / 9.0


def descriptors(padded):
    height, breadth = padded.shape
    centre = padded[4 : height - 4, 4 : breadth - 4]
    distances = []
    for offset_y, offset_x in offset_pairs:
        shifted = padded[
            4 + offset_y : height - 4 + offset_y, 4 + offset_x : breadth - 4 + offset_x
        ]
        distances.append(box_mean((centre - shifted) ** 2))
    variance = sum(distances) / 12.0 + 0.1
    return [jnp.exp(-member / variance) for member in distances]


def level_terms(fixed_padded, moving_padded, factor):
    fixed_mind = descriptors(fixed_padded)
    moving_mind = descriptors(moving_padded)
    summed = None
    for fixed_part, moving_part in zip(fixed_mind, moving_mind):
        differ = moving_part[1:-1, 1:-1] - fixed_part[1:-1, 1:-1]
        slope_y = (moving_part[2:, 1:-1] - moving_part[:-2, 1:-1]) / (2.0 * factor)
        slope_x = (moving_part[1:-1, 2:] - moving_part[1:-1, :-2]) / (2.0 * factor)
        parts = (
            differ * slope_y,
            differ * slope_x,
            slope_y * slope_y,
            slope_y * slope_x,
            slope_x * slope_x,
            differ * differ,
        )
        summed = (
            parts if summed is None else tuple((left + right for left, right in zip(summed, parts)))
        )
    return summed


def window_matrix(length, factor, cell_count):
    position = factor * jnp.arange(length, dtype=jnp.float32) + (factor - 1) / 2.0
    knots = jnp.arange(cell_count + 3, dtype=jnp.float32) - 1.0
    return bspline(position[:, None] / SPACE - knots[None, :])


def expand_mask(tissue, factor):
    side = MB // factor
    block_rows, block_cols = tissue.shape
    spread = jnp.broadcast_to(
        tissue.astype(jnp.float32)[:, None, :, None], (block_rows, side, block_cols, side)
    )
    return spread.reshape(block_rows * side, block_cols * side)


def pool_stack(images):
    planes, height, breadth = images.shape
    return images.reshape(planes, height // 2, 2, breadth // 2, 2).mean(axis=(2, 4))


def sandwich(left, values, right):
    return jnp.einsum("pa,cab,qb->cpq", left, values, right, precision=highest)


def gradient_terms(summed, weight, field):
    return jnp.stack(
        [
            weight * (summed[0] + summed[2] * field[0] + summed[3] * field[1]),
            weight * (summed[1] + summed[3] * field[0] + summed[4] * field[1]),
        ]
    )


def curvature_density(summed, weight, motion):
    return weight * (
        motion[0] * (summed[2] * motion[0] + summed[3] * motion[1])
        + motion[1] * (summed[3] * motion[0] + summed[4] * motion[1])
    )


def mismatch_of(summed, field):
    return (
        summed[5]
        + 2.0 * (summed[0] * field[0] + summed[1] * field[1])
        + field[0] * (summed[2] * field[0] + summed[3] * field[1])
        + field[1] * (summed[3] * field[0] + summed[4] * field[1])
    )


def window_of(control):
    padded = with_halo(control, (("ty", 1), ("tx", 2)), 2)
    return padded[:, 1:, 1:]


def fold_rim(padded, along, length):
    own_part = lax.slice_in_dim(padded, 4, 4 + length, axis=along)
    from_above = lax.slice_in_dim(padded, 1, 3, axis=along)
    from_below = lax.slice_in_dim(padded, length + 6, length + 7, axis=along)
    above_widths = [(0, 0), (0, 0), (0, 0)]
    above_widths[along] = (0, length - 2)
    below_widths = [(0, 0), (0, 0), (0, 0)]
    below_widths[along] = (length - 1, 0)
    return own_part + jnp.pad(from_above, above_widths) + jnp.pad(from_below, below_widths)


def run_level(padded, weight, coefficients, factor, start_zero):
    summed = level_terms(padded[0], padded[1], factor)
    height, breadth = summed[0].shape
    cells_y = height * factor // SPACE
    cells_x = breadth * factor // SPACE
    rows_window = window_matrix(height, factor, cells_y)
    cols_window = window_matrix(breadth, factor, cells_x)
    if start_zero:
        field = jnp.zeros((2, height, breadth), jnp.float32)
    else:
        field = sandwich(rows_window, window_of(coefficients), cols_window)
    for iteration in range(ITERS):
        pixel_grad = gradient_terms(summed, weight, field)
        partial_grad = sandwich(rows_window.T, pixel_grad, cols_window.T)
        spilled = with_halo(partial_grad, (("ty", 1), ("tx", 2)), 3)
        direction = fold_rim(fold_rim(spilled, 1, cells_y), 2, cells_x)
        motion = sandwich(rows_window, window_of(direction), cols_window)
        norm_sum, curvature = lax.psum(
            (jnp.sum(direction * direction), jnp.sum(curvature_density(summed, weight, motion))),
            ("ty", "tx"),
        )
        step_size = norm_sum / curvature
        coefficients = coefficients - step_size * direction
        field = field - step_size * motion
    return (coefficients, field, summed)


def shards(fixed_image, moving_image, tissue):
    stacked = jnp.stack([fixed_image, moving_image])
    fine_padded = with_halo(stacked, (("ty", 1), ("tx", 2)), HALO)
    coarse_padded = with_halo(pool_stack(stacked), (("ty", 1), ("tx", 2)), HALO)
    cells_y = fixed_image.shape[0] // SPACE
    cells_x = fixed_image.shape[1] // SPACE
    coefficients = jnp.zeros((2, cells_y, cells_x), jnp.float32)
    coefficients, field, summed = run_level(
        coarse_padded, expand_mask(tissue, 2), coefficients, 2, True
    )
    coefficients, field, summed = run_level(
        fine_padded, expand_mask(tissue, 1), coefficients, 1, False
    )
    return (coefficients, mismatch_of(summed, field))


def solution(mesh):
    placed = (P("ty", "tx"), P("ty", "tx"), P("ty", "tx"))
    return jax.shard_map(
        shards,
        mesh=mesh,
        in_specs=placed,
        out_specs=(P(None, "ty", "tx"), P("ty", "tx")),
        check_vma=False,
    )
```

profile of v0, /device:TPU:0, one launch (start us, length us, event | category | flops | bytes accessed | tf_op | source)
XLA Modules:
  0.0 384.1 jit_solution(11618381650321247970)
XLA Ops:
  0.6 6.3 %stack.52 = f32[1,32,2,128,2]{4,3,2,1,0:T(8,128)} reshape(f32[64,256]{1,0:T(8,128)} %param.4) | data formatting | bytes 131072 | tf_op jit(solution)/shard_map/stack | solution.py:191
  7.0 2.8 copy.6
  9.8 5.6 %stack.51 = f32[1,32,2,128,2]{4,3,2,1,0:T(8,128)} reshape(f32[64,256]{1,0:T(8,128)S(1)} %copy-done.1) | data formatting | bytes 131072 | tf_op jit(solution)/shard_map/stack | solution.py:191
  15.4 2.8 copy.5
  19.6 5.5 %collective-permute-start = (f32[2,6,128]{2,1,0:T(8,128)S(1)}, f32[2,6,128]{2,1,0:T(8,128)S(1)}, u32[]{:S(2)}, u32[]{:S(2)}) collective-permute-start(f32[2,6,128]{2,1,0:T(8,128)S(1)} %get-tuple-element.180), channel_id=1, source_target_pairs={{0,4},{4,8},{8,12},{12,16},{16,20},{20,24},{24,28},{1,5},{5,9},{9,... | collective-permute-start | bytes 18440 | tf_op jit(solution)/shard_map/ppermute | solution.py:34
  27.8 3.0 collective-permute-start.2
  36.6 5.4 %collective-permute-start.4 = (f32[2,3,11]{2,1,0:T(4,128)S(1)}, f32[2,3,11]{2,1,0:T(4,128)S(1)}, u32[]{:S(2)}, u32[]{:S(2)}) collective-permute-start(f32[2,3,11]{2,1,0:T(4,128)S(1)} %get-tuple-element.206), channel_id=1, source_target_pairs={{0,4},{4,8},{8,12},{12,16},{16,20},{20,24},{24,28},{1,5},{5,9},{9,... | collective-permute-start | bytes 800 | tf_op jit(solution)/shard_map/ppermute | solution.py:34
  44.7 3.1 collective-permute-start.6
  50.9 5.7 %collective-permute-start.8 = (f32[2,2,8]{2,1,0:T(2,128)S(1)}, f32[2,2,8]{2,1,0:T(2,128)S(1)}, u32[]{:S(2)}, u32[]{:S(2)}) collective-permute-start(f32[2,2,8]{2,1,0:T(2,128)S(1)} %get-tuple-element.36), channel_id=1, source_target_pairs={{0,4},{4,8},{8,12},{12,16},{16,20},{20,24},{24,28},{1,5},{5,9},{9,... | collective-permute-start | bytes 392 | tf_op jit(solution)/shard_map/ppermute | solution.py:34
  59.2 4.9 %collective-permute-start.10 = (f32[2,6,2]{2,1,0:T(8,128)S(1)}, f32[2,6,2]{2,1,0:T(8,128)S(1)}, u32[]{:S(2)}, u32[]{:S(2)}) collective-permute-start(f32[2,6,2]{2,1,0:T(8,128)S(1)} %get-tuple-element.204), channel_id=1, source_target_pairs={{0,1},{1,2},{2,3},{4,5},{5,6},{6,7},{8,9},{9,10},{10,11},{12,13},{... | collective-permute-start | bytes 296 | tf_op jit(solution)/shard_map/ppermute | solution.py:34
  66.1 47.5 %all-reduce.15 = (f32[]{:T(128)}, f32[]{:T(128)}) all-reduce(f32[]{:T(128)} %get-tuple-element.35, f32[]{:T(128)} %multiply_reduce_fusion.3), channel_id=1, replica_groups=mesh['ty'=8,'tx'=4] {'ty','tx'}, use_global_device_ids=true, to_apply=%region_2.3 | all-reduce | flops 2 | bytes 16 | tf_op jit(solution)/shard_map/psum | solution.py:180
  116.7 4.8 %collective-permute-start.12 = (f32[2,3,11]{2,1,0:T(4,128)S(1)}, f32[2,3,11]{2,1,0:T(4,128)S(1)}, u32[]{:S(2)}, u32[]{:S(2)}) collective-permute-start(f32[2,3,11]{2,1,0:T(4,128)S(1)} %get-tuple-element.202), channel_id=1, source_target_pairs={{0,4},{4,8},{8,12},{12,16},{16,20},{20,24},{24,28},{1,5},{5,9},{9,... | collective-permute-start | bytes 800 | tf_op jit(solution)/shard_map/ppermute | solution.py:34
  122.9 5.5 %collective-permute-start.20 = (f32[2,6,256]{2,1,0:T(8,128)S(1)}, f32[2,6,256]{2,1,0:T(8,128)S(1)}, u32[]{:S(2)}, u32[]{:S(2)}) collective-permute-start(f32[2,6,256]{2,1,0:T(8,128)S(1)} %get-tuple-element.102), channel_id=1, source_target_pairs={{0,4},{4,8},{8,12},{12,16},{16,20},{20,24},{24,28},{1,5},{5,9},{9,... | collective-permute-start | bytes 36872 | tf_op jit(solution)/shard_map/ppermute | solution.py:34
  129.7 3.0 collective-permute-start.14
  135.8 5.4 %collective-permute-start.16 = (f32[2,2,8]{2,1,0:T(2,128)S(1)}, f32[2,2,8]{2,1,0:T(2,128)S(1)}, u32[]{:S(2)}, u32[]{:S(2)}) collective-permute-start(f32[2,2,8]{2,1,0:T(2,128)S(1)} %get-tuple-element.34), channel_id=1, source_target_pairs={{0,4},{4,8},{8,12},{12,16},{16,20},{20,24},{24,28},{1,5},{5,9},{9,... | collective-permute-start | bytes 392 | tf_op jit(solution)/shard_map/ppermute | solution.py:34
  143.9 3.4 collective-permute-start.18
  149.3 46.0 %all-reduce.14 = (f32[]{:T(128)}, f32[]{:T(128)}) all-reduce(f32[]{:T(128)} %get-tuple-element.33, f32[]{:T(128)} %multiply_reduce_fusion.2), channel_id=1, replica_groups=mesh['ty'=8,'tx'=4] {'ty','tx'}, use_global_device_ids=true, to_apply=%region_6.7 | all-reduce | flops 2 | bytes 16 | tf_op jit(solution)/shard_map/psum | solution.py:180
  198.0 4.8 %collective-permute-start.24 = (f32[2,2,8]{2,1,0:T(2,128)S(1)}, f32[2,2,8]{2,1,0:T(2,128)S(1)}, u32[]{:S(2)}, u32[]{:S(2)}) collective-permute-start(f32[2,2,8]{2,1,0:T(2,128)S(1)} %multiply_subtract_fusion.4), channel_id=1, source_target_pairs={{0,4},{4,8},{8,12},{12,16},{16,20},{20,24},{24,28},{1,5},{5,9},{9,... | collective-permute-start | bytes 392 | tf_op jit(solution)/shard_map/ppermute | solution.py:34
  205.5 3.0 collective-permute-start.26
  211.0 4.5 %collective-permute-start.22 = (f32[2,76,6]{2,1,0:T(8,128)S(1)}, f32[2,76,6]{2,1,0:T(8,128)S(1)}, u32[]{:S(2)}, u32[]{:S(2)}) collective-permute-start(f32[2,76,6]{2,1,0:T(8,128)S(1)} %get-tuple-element.100), channel_id=1, source_target_pairs={{0,1},{1,2},{2,3},{4,5},{5,6},{6,7},{8,9},{9,10},{10,11},{12,13},{... | collective-permute-start | bytes 10952 | tf_op jit(solution)/shard_map/ppermute | solution.py:34
  217.4 2.1 divide_exponential_fusion
  219.7 2.1 multiply_add_fusion
  225.3 5.4 %collective-permute-start.28 = (f32[2,3,11]{2,1,0:T(4,128)S(1)}, f32[2,3,11]{2,1,0:T(4,128)S(1)}, u32[]{:S(2)}, u32[]{:S(2)}) collective-permute-start(f32[2,3,11]{2,1,0:T(4,128)S(1)} %get-tuple-element.196), channel_id=1, source_target_pairs={{0,4},{4,8},{8,12},{12,16},{16,20},{20,24},{24,28},{1,5},{5,9},{9,... | collective-permute-start | bytes 800 | tf_op jit(solution)/shard_map/ppermute | solution.py:34
  233.4 4.5 %collective-permute-start.30 = (f32[2,11,3]{2,1,0:T(8,128)S(1)}, f32[2,11,3]{2,1,0:T(8,128)S(1)}, u32[]{:S(2)}, u32[]{:S(2)}) collective-permute-start(f32[2,11,3]{2,1,0:T(8,128)S(1)} %get-tuple-element.184), channel_id=1, source_target_pairs={{0,1},{1,2},{2,3},{4,5},{5,6},{6,7},{8,9},{9,10},{10,11},{12,13},{... | collective-permute-start | bytes 800 | tf_op jit(solution)/shard_map/ppermute | solution.py:34
  241.0 5.7 %collective-permute-start.32 = (f32[2,2,8]{2,1,0:T(2,128)S(1)}, f32[2,2,8]{2,1,0:T(2,128)S(1)}, u32[]{:S(2)}, u32[]{:S(2)}) collective-permute-start(f32[2,2,8]{2,1,0:T(2,128)S(1)} %get-tuple-element.13), channel_id=1, source_target_pairs={{0,4},{4,8},{8,12},{12,16},{16,20},{20,24},{24,28},{1,5},{5,9},{9,... | collective-permute-start | bytes 392 | tf_op jit(solution)/shard_map/ppermute | solution.py:34
  249.3 4.9 %collective-permute-start.34 = (f32[2,6,2]{2,1,0:T(8,128)S(1)}, f32[2,6,2]{2,1,0:T(8,128)S(1)}, u32[]{:S(2)}, u32[]{:S(2)}) collective-permute-start(f32[2,6,2]{2,1,0:T(8,128)S(1)} %get-tuple-element.194), channel_id=1, source_target_pairs={{0,1},{1,2},{2,3},{4,5},{5,6},{6,7},{8,9},{9,10},{10,11},{12,13},{... | collective-permute-start | bytes 296 | tf_op jit(solution)/shard_map/ppermute | solution.py:34
  256.4 47.4 %all-reduce.13 = (f32[]{:T(128)}, f32[]{:T(128)}) all-reduce(f32[]{:T(128)} %get-tuple-element.12, f32[]{:T(128)} %multiply_reduce_fusion.1), channel_id=1, replica_groups=mesh['ty'=8,'tx'=4] {'ty','tx'}, use_global_device_ids=true, to_apply=%region_10.11 | all-reduce | flops 2 | bytes 16 | tf_op jit(solution)/shard_map/psum | solution.py:180
  306.9 4.8 %collective-permute-start.36 = (f32[2,3,11]{2,1,0:T(4,128)S(1)}, f32[2,3,11]{2,1,0:T(4,128)S(1)}, u32[]{:S(2)}, u32[]{:S(2)}) collective-permute-start(f32[2,3,11]{2,1,0:T(4,128)S(1)} %get-tuple-element.192), channel_id=1, source_target_pairs={{0,4},{4,8},{8,12},{12,16},{16,20},{20,24},{24,28},{1,5},{5,9},{9,... | collective-permute-start | bytes 800 | tf_op jit(solution)/shard_map/ppermute | solution.py:34
  314.4 3.0 collective-permute-start.38
  320.5 5.4 %collective-permute-start.40 = (f32[2,2,8]{2,1,0:T(2,128)S(1)}, f32[2,2,8]{2,1,0:T(2,128)S(1)}, u32[]{:S(2)}, u32[]{:S(2)}) collective-permute-start(f32[2,2,8]{2,1,0:T(2,128)S(1)} %get-tuple-element.11), channel_id=1, source_target_pairs={{0,4},{4,8},{8,12},{12,16},{16,20},{20,24},{24,28},{1,5},{5,9},{9,... | collective-permute-start | bytes 392 | tf_op jit(solution)/shard_map/ppermute | solution.py:34
  328.6 3.5 collective-permute-start.42
  334.2 47.2 %all-reduce.12 = (f32[]{:T(128)}, f32[]{:T(128)}) all-reduce(f32[]{:T(128)} %get-tuple-element.10, f32[]{:T(128)} %multiply_reduce_fusion), channel_id=1, replica_groups=mesh['ty'=8,'tx'=4] {'ty','tx'}, use_global_device_ids=true, to_apply=%region_14.15 | all-reduce | flops 2 | bytes 16 | tf_op jit(solution)/shard_map/psum | solution.py:180
  (177 shorter events, 67.6 us)
Async XLA Ops:
  18.3 6.8 %collective-permute-start.1 = (f32[2,6,128]{2,1,0:T(8,128)S(1)}, f32[2,6,128]{2,1,0:T(8,128)S(1)}, u32[]{:S(2)}, u32[]{:S(2)}) collective-permute-start(f32[2,6,128]{2,1,0:T(8,128)S(1)} %get-tuple-element.181), channel_id=1, source_target_pairs={{4,0},{8,4},{12,8},{16,12},{20,16},{24,20},{28,24},{5,1},{9,5},{13... | collective-permute-start | bytes 18440 | tf_op jit(solution)/shard_map/ppermute | solution.py:37
  19.6 6.8 %collective-permute-start = (f32[2,6,128]{2,1,0:T(8,128)S(1)}, f32[2,6,128]{2,1,0:T(8,128)S(1)}, u32[]{:S(2)}, u32[]{:S(2)}) collective-permute-start(f32[2,6,128]{2,1,0:T(8,128)S(1)} %get-tuple-element.180), channel_id=1, source_target_pairs={{0,4},{4,8},{8,12},{12,16},{16,20},{20,24},{24,28},{1,5},{5,9},{9,... | collective-permute-start | bytes 18440 | tf_op jit(solution)/shard_map/ppermute | solution.py:34
  35.3 6.8 %collective-permute-start.5 = (f32[2,3,11]{2,1,0:T(4,128)S(1)}, f32[2,3,11]{2,1,0:T(4,128)S(1)}, u32[]{:S(2)}, u32[]{:S(2)}) collective-permute-start(f32[2,3,11]{2,1,0:T(4,128)S(1)} %get-tuple-element.207), channel_id=1, source_target_pairs={{4,0},{8,4},{12,8},{16,12},{20,16},{24,20},{28,24},{5,1},{9,5},{13... | collective-permute-start | bytes 800 | tf_op jit(solution)/shard_map/ppermute | solution.py:37
  36.6 6.8 %collective-permute-start.4 = (f32[2,3,11]{2,1,0:T(4,128)S(1)}, f32[2,3,11]{2,1,0:T(4,128)S(1)}, u32[]{:S(2)}, u32[]{:S(2)}) collective-permute-start(f32[2,3,11]{2,1,0:T(4,128)S(1)} %get-tuple-element.206), channel_id=1, source_target_pairs={{0,4},{4,8},{8,12},{12,16},{16,20},{20,24},{24,28},{1,5},{5,9},{9,... | collective-permute-start | bytes 800 | tf_op jit(solution)/shard_map/ppermute | solution.py:34
  49.6 7.0 %collective-permute-start.9 = (f32[2,2,8]{2,1,0:T(2,128)S(1)}, f32[2,2,8]{2,1,0:T(2,128)S(1)}, u32[]{:S(2)}, u32[]{:S(2)}) collective-permute-start(f32[2,2,8]{2,1,0:T(2,128)S(1)} %get-tuple-element.36), channel_id=1, source_target_pairs={{4,0},{8,4},{12,8},{16,12},{20,16},{24,20},{28,24},{5,1},{9,5},{13... | collective-permute-start | bytes 392 | tf_op jit(solution)/shard_map/ppermute | solution.py:37
  50.9 7.0 %collective-permute-start.8 = (f32[2,2,8]{2,1,0:T(2,128)S(1)}, f32[2,2,8]{2,1,0:T(2,128)S(1)}, u32[]{:S(2)}, u32[]{:S(2)}) collective-permute-start(f32[2,2,8]{2,1,0:T(2,128)S(1)} %get-tuple-element.36), channel_id=1, source_target_pairs={{0,4},{4,8},{8,12},{12,16},{16,20},{20,24},{24,28},{1,5},{5,9},{9,... | collective-permute-start | bytes 392 | tf_op jit(solution)/shard_map/ppermute | solution.py:34
  58.0 6.2 %collective-permute-start.11 = (f32[2,6,2]{2,1,0:T(8,128)S(1)}, f32[2,6,2]{2,1,0:T(8,128)S(1)}, u32[]{:S(2)}, u32[]{:S(2)}) collective-permute-start(f32[2,6,2]{2,1,0:T(8,128)S(1)} %get-tuple-element.205), channel_id=1, source_target_pairs={{1,0},{2,1},{3,2},{5,4},{6,5},{7,6},{9,8},{10,9},{11,10},{13,12},{... | collective-permute-start | bytes 296 | tf_op jit(solution)/shard_map/ppermute | solution.py:37
  59.2 5.7 %collective-permute-start.10 = (f32[2,6,2]{2,1,0:T(8,128)S(1)}, f32[2,6,2]{2,1,0:T(8,128)S(1)}, u32[]{:S(2)}, u32[]{:S(2)}) collective-permute-start(f32[2,6,2]{2,1,0:T(8,128)S(1)} %get-tuple-element.204), channel_id=1, source_target_pairs={{0,1},{1,2},{2,3},{4,5},{5,6},{6,7},{8,9},{9,10},{10,11},{12,13},{... | collective-permute-start | bytes 296 | tf_op jit(solution)/shard_map/ppermute | solution.py:34
  115.4 12.9 %collective-permute-start.13 = (f32[2,3,11]{2,1,0:T(4,128)S(1)}, f32[2,3,11]{2,1,0:T(4,128)S(1)}, u32[]{:S(2)}, u32[]{:S(2)}) collective-permute-start(f32[2,3,11]{2,1,0:T(4,128)S(1)} %get-tuple-element.203), channel_id=1, source_target_pairs={{4,0},{8,4},{12,8},{16,12},{20,16},{24,20},{28,24},{5,1},{9,5},{13... | collective-permute-start | bytes 800 | tf_op jit(solution)/shard_map/ppermute | solution.py:37
  116.7 11.6 %collective-permute-start.12 = (f32[2,3,11]{2,1,0:T(4,128)S(1)}, f32[2,3,11]{2,1,0:T(4,128)S(1)}, u32[]{:S(2)}, u32[]{:S(2)}) collective-permute-start(f32[2,3,11]{2,1,0:T(4,128)S(1)} %get-tuple-element.202), channel_id=1, source_target_pairs={{0,4},{4,8},{8,12},{12,16},{16,20},{20,24},{24,28},{1,5},{5,9},{9,... | collective-permute-start | bytes 800 | tf_op jit(solution)/shard_map/ppermute | solution.py:34
  121.6 88.0 %collective-permute-start.21 = (f32[2,6,256]{2,1,0:T(8,128)S(1)}, f32[2,6,256]{2,1,0:T(8,128)S(1)}, u32[]{:S(2)}, u32[]{:S(2)}) collective-permute-start(f32[2,6,256]{2,1,0:T(8,128)S(1)} %get-tuple-element.103), channel_id=1, source_target_pairs={{4,0},{8,4},{12,8},{16,12},{20,16},{24,20},{28,24},{5,1},{9,5},{13... | collective-permute-start | bytes 36872 | tf_op jit(solution)/shard_map/ppermute | solution.py:37
  122.9 86.7 %collective-permute-start.20 = (f32[2,6,256]{2,1,0:T(8,128)S(1)}, f32[2,6,256]{2,1,0:T(8,128)S(1)}, u32[]{:S(2)}, u32[]{:S(2)}) collective-permute-start(f32[2,6,256]{2,1,0:T(8,128)S(1)} %get-tuple-element.102), channel_id=1, source_target_pairs={{0,4},{4,8},{8,12},{12,16},{16,20},{20,24},{24,28},{1,5},{5,9},{9,... | collective-permute-start | bytes 36872 | tf_op jit(solution)/shard_map/ppermute | solution.py:34
  134.5 6.8 %collective-permute-start.17 = (f32[2,2,8]{2,1,0:T(2,128)S(1)}, f32[2,2,8]{2,1,0:T(2,128)S(1)}, u32[]{:S(2)}, u32[]{:S(2)}) collective-permute-start(f32[2,2,8]{2,1,0:T(2,128)S(1)} %get-tuple-element.34), channel_id=1, source_target_pairs={{4,0},{8,4},{12,8},{16,12},{20,16},{24,20},{28,24},{5,1},{9,5},{13... | collective-permute-start | bytes 392 | tf_op jit(solution)/shard_map/ppermute | solution.py:37
  135.8 6.7 %collective-permute-start.16 = (f32[2,2,8]{2,1,0:T(2,128)S(1)}, f32[2,2,8]{2,1,0:T(2,128)S(1)}, u32[]{:S(2)}, u32[]{:S(2)}) collective-permute-start(f32[2,2,8]{2,1,0:T(2,128)S(1)} %get-tuple-element.34), channel_id=1, source_target_pairs={{0,4},{4,8},{8,12},{12,16},{16,20},{20,24},{24,28},{1,5},{5,9},{9,... | collective-permute-start | bytes 392 | tf_op jit(solution)/shard_map/ppermute | solution.py:34
  142.6 4.7 %collective-permute-start.19 = (f32[2,6,2]{2,1,0:T(8,128)S(1)}, f32[2,6,2]{2,1,0:T(8,128)S(1)}, u32[]{:S(2)}, u32[]{:S(2)}) collective-permute-start(f32[2,6,2]{2,1,0:T(8,128)S(1)} %get-tuple-element.201), channel_id=1, source_target_pairs={{1,0},{2,1},{3,2},{5,4},{6,5},{7,6},{9,8},{10,9},{11,10},{13,12},{... | collective-permute-start | bytes 296 | tf_op jit(solution)/shard_map/ppermute | solution.py:37
  196.7 6.3 %collective-permute-start.25 = (f32[2,2,8]{2,1,0:T(2,128)S(1)}, f32[2,2,8]{2,1,0:T(2,128)S(1)}, u32[]{:S(2)}, u32[]{:S(2)}) collective-permute-start(f32[2,2,8]{2,1,0:T(2,128)S(1)} %multiply_subtract_fusion.4), channel_id=1, source_target_pairs={{4,0},{8,4},{12,8},{16,12},{20,16},{24,20},{28,24},{5,1},{9,5},{13... | collective-permute-start | bytes 392 | tf_op jit(solution)/shard_map/ppermute | solution.py:37
  198.0 6.1 %collective-permute-start.24 = (f32[2,2,8]{2,1,0:T(2,128)S(1)}, f32[2,2,8]{2,1,0:T(2,128)S(1)}, u32[]{:S(2)}, u32[]{:S(2)}) collective-permute-start(f32[2,2,8]{2,1,0:T(2,128)S(1)} %multiply_subtract_fusion.4), channel_id=1, source_target_pairs={{0,4},{4,8},{8,12},{12,16},{16,20},{20,24},{24,28},{1,5},{5,9},{9,... | collective-permute-start | bytes 392 | tf_op jit(solution)/shard_map/ppermute | solution.py:34
  209.7 6.2 %collective-permute-start.23 = (f32[2,76,6]{2,1,0:T(8,128)S(1)}, f32[2,76,6]{2,1,0:T(8,128)S(1)}, u32[]{:S(2)}, u32[]{:S(2)}) collective-permute-start(f32[2,76,6]{2,1,0:T(8,128)S(1)} %get-tuple-element.101), channel_id=1, source_target_pairs={{1,0},{2,1},{3,2},{5,4},{6,5},{7,6},{9,8},{10,9},{11,10},{13,12},{... | collective-permute-start | bytes 10952 | tf_op jit(solution)/shard_map/ppermute | solution.py:37
  211.0 5.2 %collective-permute-start.22 = (f32[2,76,6]{2,1,0:T(8,128)S(1)}, f32[2,76,6]{2,1,0:T(8,128)S(1)}, u32[]{:S(2)}, u32[]{:S(2)}) collective-permute-start(f32[2,76,6]{2,1,0:T(8,128)S(1)} %get-tuple-element.100), channel_id=1, source_target_pairs={{0,1},{1,2},{2,3},{4,5},{5,6},{6,7},{8,9},{9,10},{10,11},{12,13},{... | collective-permute-start | bytes 10952 | tf_op jit(solution)/shard_map/ppermute | solution.py:34
  224.0 6.7 %collective-permute-start.29 = (f32[2,3,11]{2,1,0:T(4,128)S(1)}, f32[2,3,11]{2,1,0:T(4,128)S(1)}, u32[]{:S(2)}, u32[]{:S(2)}) collective-permute-start(f32[2,3,11]{2,1,0:T(4,128)S(1)} %get-tuple-element.197), channel_id=1, source_target_pairs={{4,0},{8,4},{12,8},{16,12},{20,16},{24,20},{28,24},{5,1},{9,5},{13... | collective-permute-start | bytes 800 | tf_op jit(solution)/shard_map/ppermute | solution.py:37
  225.3 6.7 %collective-permute-start.28 = (f32[2,3,11]{2,1,0:T(4,128)S(1)}, f32[2,3,11]{2,1,0:T(4,128)S(1)}, u32[]{:S(2)}, u32[]{:S(2)}) collective-permute-start(f32[2,3,11]{2,1,0:T(4,128)S(1)} %get-tuple-element.196), channel_id=1, source_target_pairs={{0,4},{4,8},{8,12},{12,16},{16,20},{20,24},{24,28},{1,5},{5,9},{9,... | collective-permute-start | bytes 800 | tf_op jit(solution)/shard_map/ppermute | solution.py:34
  232.1 5.8 %collective-permute-start.31 = (f32[2,11,3]{2,1,0:T(8,128)S(1)}, f32[2,11,3]{2,1,0:T(8,128)S(1)}, u32[]{:S(2)}, u32[]{:S(2)}) collective-permute-start(f32[2,11,3]{2,1,0:T(8,128)S(1)} %get-tuple-element.185), channel_id=1, source_target_pairs={{1,0},{2,1},{3,2},{5,4},{6,5},{7,6},{9,8},{10,9},{11,10},{13,12},{... | collective-permute-start | bytes 800 | tf_op jit(solution)/shard_map/ppermute | solution.py:37
  233.4 5.4 %collective-permute-start.30 = (f32[2,11,3]{2,1,0:T(8,128)S(1)}, f32[2,11,3]{2,1,0:T(8,128)S(1)}, u32[]{:S(2)}, u32[]{:S(2)}) collective-permute-start(f32[2,11,3]{2,1,0:T(8,128)S(1)} %get-tuple-element.184), channel_id=1, source_target_pairs={{0,1},{1,2},{2,3},{4,5},{5,6},{6,7},{8,9},{9,10},{10,11},{12,13},{... | collective-permute-start | bytes 800 | tf_op jit(solution)/shard_map/ppermute | solution.py:34
  239.7 7.0 %collective-permute-start.33 = (f32[2,2,8]{2,1,0:T(2,128)S(1)}, f32[2,2,8]{2,1,0:T(2,128)S(1)}, u32[]{:S(2)}, u32[]{:S(2)}) collective-permute-start(f32[2,2,8]{2,1,0:T(2,128)S(1)} %get-tuple-element.13), channel_id=1, source_target_pairs={{4,0},{8,4},{12,8},{16,12},{20,16},{24,20},{28,24},{5,1},{9,5},{13... | collective-permute-start | bytes 392 | tf_op jit(solution)/shard_map/ppermute | solution.py:37
  241.0 7.0 %collective-permute-start.32 = (f32[2,2,8]{2,1,0:T(2,128)S(1)}, f32[2,2,8]{2,1,0:T(2,128)S(1)}, u32[]{:S(2)}, u32[]{:S(2)}) collective-permute-start(f32[2,2,8]{2,1,0:T(2,128)S(1)} %get-tuple-element.13), channel_id=1, source_target_pairs={{0,4},{4,8},{8,12},{12,16},{16,20},{20,24},{24,28},{1,5},{5,9},{9,... | collective-permute-start | bytes 392 | tf_op jit(solution)/shard_map/ppermute | solution.py:34
  248.1 6.2 %collective-permute-start.35 = (f32[2,6,2]{2,1,0:T(8,128)S(1)}, f32[2,6,2]{2,1,0:T(8,128)S(1)}, u32[]{:S(2)}, u32[]{:S(2)}) collective-permute-start(f32[2,6,2]{2,1,0:T(8,128)S(1)} %get-tuple-element.195), channel_id=1, source_target_pairs={{1,0},{2,1},{3,2},{5,4},{6,5},{7,6},{9,8},{10,9},{11,10},{13,12},{... | collective-permute-start | bytes 296 | tf_op jit(solution)/shard_map/ppermute | solution.py:37
  249.3 5.8 %collective-permute-start.34 = (f32[2,6,2]{2,1,0:T(8,128)S(1)}, f32[2,6,2]{2,1,0:T(8,128)S(1)}, u32[]{:S(2)}, u32[]{:S(2)}) collective-permute-start(f32[2,6,2]{2,1,0:T(8,128)S(1)} %get-tuple-element.194), channel_id=1, source_target_pairs={{0,1},{1,2},{2,3},{4,5},{5,6},{6,7},{8,9},{9,10},{10,11},{12,13},{... | collective-permute-start | bytes 296 | tf_op jit(solution)/shard_map/ppermute | solution.py:34
  305.6 6.1 %collective-permute-start.37 = (f32[2,3,11]{2,1,0:T(4,128)S(1)}, f32[2,3,11]{2,1,0:T(4,128)S(1)}, u32[]{:S(2)}, u32[]{:S(2)}) collective-permute-start(f32[2,3,11]{2,1,0:T(4,128)S(1)} %get-tuple-element.193), channel_id=1, source_target_pairs={{4,0},{8,4},{12,8},{16,12},{20,16},{24,20},{28,24},{5,1},{9,5},{13... | collective-permute-start | bytes 800 | tf_op jit(solution)/shard_map/ppermute | solution.py:37
  306.9 6.1 %collective-permute-start.36 = (f32[2,3,11]{2,1,0:T(4,128)S(1)}, f32[2,3,11]{2,1,0:T(4,128)S(1)}, u32[]{:S(2)}, u32[]{:S(2)}) collective-permute-start(f32[2,3,11]{2,1,0:T(4,128)S(1)} %get-tuple-element.192), channel_id=1, source_target_pairs={{0,4},{4,8},{8,12},{12,16},{16,20},{20,24},{24,28},{1,5},{5,9},{9,... | collective-permute-start | bytes 800 | tf_op jit(solution)/shard_map/ppermute | solution.py:34
  319.2 6.7 %collective-permute-start.41 = (f32[2,2,8]{2,1,0:T(2,128)S(1)}, f32[2,2,8]{2,1,0:T(2,128)S(1)}, u32[]{:S(2)}, u32[]{:S(2)}) collective-permute-start(f32[2,2,8]{2,1,0:T(2,128)S(1)} %get-tuple-element.11), channel_id=1, source_target_pairs={{4,0},{8,4},{12,8},{16,12},{20,16},{24,20},{28,24},{5,1},{9,5},{13... | collective-permute-start | bytes 392 | tf_op jit(solution)/shard_map/ppermute | solution.py:37
  320.5 6.7 %collective-permute-start.40 = (f32[2,2,8]{2,1,0:T(2,128)S(1)}, f32[2,2,8]{2,1,0:T(2,128)S(1)}, u32[]{:S(2)}, u32[]{:S(2)}) collective-permute-start(f32[2,2,8]{2,1,0:T(2,128)S(1)} %get-tuple-element.11), channel_id=1, source_target_pairs={{0,4},{4,8},{8,12},{12,16},{16,20},{20,24},{24,28},{1,5},{5,9},{9,... | collective-permute-start | bytes 392 | tf_op jit(solution)/shard_map/ppermute | solution.py:34
  327.3 4.8 %collective-permute-start.43 = (f32[2,6,2]{2,1,0:T(8,128)S(1)}, f32[2,6,2]{2,1,0:T(8,128)S(1)}, u32[]{:S(2)}, u32[]{:S(2)}) collective-permute-start(f32[2,6,2]{2,1,0:T(8,128)S(1)} %get-tuple-element.191), channel_id=1, source_target_pairs={{1,0},{2,1},{3,2},{5,4},{6,5},{7,6},{9,8},{10,9},{11,10},{13,12},{... | collective-permute-start | bytes 296 | tf_op jit(solution)/shard_map/ppermute | solution.py:37
  (15 other events, 103.5 us)
where the time goes:
time: 386 us; the launch traced here: 384 us
  blocking collectives  188 us (49%)
  starting transfers between devices  128 us (33%)
  waiting for transfers between devices  19.6 us (5%)
  local copies, waits for them, and re-layouts  19.5 us (5%)
  other arithmetic  17.5 us (5%)
  between operations  6.96 us (2%)
  matrix products  4.67 us (1%)
    psum x4, blocking collectives, run_level(): lax.psum((jnp.sum(direction * direction), jnp.sum(curvature_density(summe...  188 us
    ppermute x22, starting transfers between devices, with_halo(): lax.ppermute(lax.slice_in_dim(block, block.shape[dim] - width, None, axis...  99.5 us
    ppermute x22, starting transfers between devices, with_halo(): lax.ppermute(lax.slice_in_dim(block, 0, width, axis=dim), axis, backward)  28.3 us
    ppermute x22, waiting for transfers between devices, with_halo(): lax.ppermute(lax.slice_in_dim(block, block.shape[dim] - width, None, axis...  19.5 us
    another operation x4, local copies, waits for them, and re-layouts, shards(): stacked = jnp.stack([fixed_image, moving_image])  17.6 us
  transfers between devices with their start and end apart: 44, of which 20 were waited for; matrix products, arithmetic and copies ran while one was open for 1% of the time, Pallas kernels for 0%

commit v1 on v0

v1 whole, which is shorter than its diff:
```python
import functools

import jax
import jax.numpy as jnp
from jax import lax
from jax.experimental import pallas as pl
from jax.experimental.pallas import tpu as pltpu
from jax.sharding import PartitionSpec as P

SPACE = 32
REACH_Y = 5
REACH_X = 11
RIM = 16
MESH = pl.DeviceIdType.MESH
F32 = jnp.float32

half_offsets = ((0, 2), (2, 0), (2, 2), (2, -2), (0, 4), (4, 0))
travels = ((-1, 0), (1, 0), (0, -1), (0, 1), (-1, -1), (-1, 1), (1, -1), (1, 1))


def bspline(values):
    magnitude = jnp.abs(values)
    near_part = 2.0 / 3.0 - magnitude * magnitude + 0.5 * magnitude * magnitude * magnitude
    rest = 2.0 - magnitude
    far_part = rest * rest * rest / 6.0
    return jnp.where(magnitude < 1.0, near_part, jnp.where(magnitude < 2.0, far_part, 0.0))


def moved(values, by_y, by_x):
    rows, lanes = values.shape
    if by_x:
        values = pltpu.roll(values, (-by_x) % lanes, 1)
    if by_y:
        values = pltpu.roll(values, (-by_y) % rows, 0)
    return values


def minds_into(image, lane_step, out_ref):
    total = None
    for index, (offset_y, offset_x) in enumerate(half_offsets):
        gap = image - moved(image, offset_y, lane_step * offset_x)
        square = gap * gap
        rows = square + moved(square, 1, 0) + moved(square, -1, 0)
        box = rows + moved(rows, 0, lane_step) + moved(rows, 0, -lane_step)
        other = moved(box, -offset_y, -lane_step * offset_x)
        out_ref[2 * index, : image.shape[0]] = box
        out_ref[2 * index + 1, : image.shape[0]] = other
        both = box + other
        total = both if total is None else total + both
    return -1.0 / (total / 12.0 + 0.9)


def terms_into(fixed, moving, lane_step, factor, fixed_ref, moving_ref, terms_ref, wide):
    rows = fixed.shape[0]
    height = rows - 16
    fixed_scale = minds_into(fixed, lane_step, fixed_ref)[8 : 8 + height, :wide]
    moving_scale = minds_into(moving, lane_step, moving_ref)
    sums = None
    for index in range(12):
        fixed_mind = jnp.exp(fixed_ref[index, 8 : 8 + height, :wide] * fixed_scale)
        mind = jnp.exp(moving_ref[index, :rows] * moving_scale)
        differ = mind[8 : 8 + height, :wide] - fixed_mind
        slope_y = moved(mind[:, :wide], 1, 0) - moved(mind[:, :wide], -1, 0)
        slope_y = slope_y[8 : 8 + height]
        own = mind[8 : 8 + height]
        slope_x = (moved(own, 0, lane_step) - moved(own, 0, -lane_step))[:, :wide]
        parts = (
            differ * slope_y,
            differ * slope_x,
            slope_y * slope_y,
            slope_y * slope_x,
            slope_x * slope_x,
            differ * differ,
        )
        sums = parts if sums is None else tuple(a + b for a, b in zip(sums, parts))
    once = 1.0 / (2.0 * factor)
    scales = (once, once, once * once, once * once, once * once, 1.0)
    for index in range(6):
        terms_ref[index] = sums[index] * scales[index]


def kernel(
    count_y,
    count_x,
    widths,
    tissue_ref,
    fixed_ref,
    moving_ref,
    coef_ref,
    mismatch_ref,
    mid,
    left_side,
    right_side,
    full,
    fixed_minds,
    moving_minds,
    fine_terms,
    coarse_terms,
    fine_weight,
    coarse_weight,
    fine_rows,
    coarse_rows,
    fine_cols,
    coarse_cols,
    grid_sum,
    *rest,
):
    rounds = len(widths)
    boxes = rest[:rounds]
    rim_send, rim_recv, send_sem, recv_sem = rest[rounds:]
    ty = lax.axis_index("ty")
    tx = lax.axis_index("tx")
    count = count_y * count_x
    me = ty * count_x + tx
    height, breadth = fixed_ref.shape
    knots = count_x * (breadth // SPACE)
    cells_y, cells_x = height // SPACE, breadth // SPACE

    def peer(step):
        other = lax.rem(me + step, count)
        return (other // count_x, lax.rem(other, count_x))

    def for_peers(act):
        if count <= 64:
            for step in range(1, count):
                act(peer(step))
        else:

            def body(step, carry):
                act(peer(step))
                return carry

            lax.fori_loop(1, count, body, 0)

    low, high = slice(0, RIM), slice(RIM + height, 2 * RIM + height)

    @pl.when(ty == 0)
    def _():
        for ref in (mid, left_side, right_side):
            ref[:, low] = jnp.zeros((2, RIM, ref.shape[2]), F32)

    @pl.when(ty == count_y - 1)
    def _():
        for ref in (mid, left_side, right_side):
            ref[:, high] = jnp.zeros((2, RIM, ref.shape[2]), F32)

    @pl.when(tx == 0)
    def _():
        left_side[...] = jnp.zeros(left_side.shape, F32)

    @pl.when(tx == count_x - 1)
    def _():
        right_side[...] = jnp.zeros(right_side.shape, F32)

    barrier = pltpu.get_barrier_semaphore()
    for_peers(
        lambda device: pl.semaphore_signal(barrier, 1, device_id=device, device_id_type=MESH)
    )

    lane = lax.broadcasted_iota(jnp.int32, (8, breadth), 1)
    for k in range(REACH_X):
        fine_cols[k] = bspline(lane.astype(F32) / SPACE - (k - 1.0))
        coarse_cols[k] = bspline((lane.astype(F32) + 0.5) / SPACE - (k - 1.0))
    row = lax.broadcasted_iota(jnp.int32, (height, 128), 0).astype(F32)
    coarse_row = lax.broadcasted_iota(jnp.int32, (height // 2, 128), 0).astype(F32)
    for r in range(REACH_Y):
        fine_rows[r] = bspline(row / SPACE - (r - 1.0))
        coarse_rows[r] = bspline((2.0 * coarse_row + 0.5) / SPACE - (r - 1.0))
    even = lax.rem(lane, 2) == 0
    for i in range(cells_y):
        line = jnp.zeros((8, breadth), F32)
        for j in range(cells_x):
            value = tissue_ref[i, j].astype(F32)
            inside = (lane >= j * SPACE) & (lane < (j + 1) * SPACE)
            line = jnp.where(inside, value, line)
        half = jnp.where(even, line, 0.0)
        for part in range(SPACE // 8):
            start = i * SPACE + part * 8
            fine_weight[start : start + 8] = line
        for part in range(SPACE // 16):
            start = i * (SPACE // 2) + part * 8
            coarse_weight[start : start + 8] = half

    pl.semaphore_wait(barrier, count - 1)

    def rows_of(travel):
        if travel == 0:
            return slice(0, height), slice(RIM, RIM + height)
        if travel > 0:
            return slice(height - RIM, height), low
        return slice(0, RIM), high

    def landing(travel_y, travel_x):
        ref = mid if travel_x == 0 else (left_side if travel_x > 0 else right_side)
        return ref.at[:, rows_of(travel_y)[1]]

    def exists(travel_y, travel_x):
        to_y, to_x = ty + travel_y, tx + travel_x
        return (to_y >= 0) & (to_y < count_y) & (to_x >= 0) & (to_x < count_x)

    for index, (travel_y, travel_x) in enumerate(travels):

        @pl.when(exists(travel_y, travel_x))
        def _():
            source_rows = rows_of(travel_y)[0]
            if travel_x == 0:
                lanes = slice(0, breadth)
            elif travel_x > 0:
                lanes = slice(breadth - 128, breadth)
            else:
                lanes = slice(0, 128)
            for image, ref in enumerate((fixed_ref, moving_ref)):
                pltpu.make_async_remote_copy(
                    src_ref=ref.at[source_rows, lanes],
                    dst_ref=landing(travel_y, travel_x).at[image],
                    send_sem=rim_send.at[index],
                    recv_sem=rim_recv.at[index],
                    device_id=(ty + travel_y, tx + travel_x),
                    device_id_type=MESH,
                ).start()

    for image, ref in enumerate((fixed_ref, moving_ref)):
        mid[image, RIM : RIM + height] = ref[...]

    for index, (travel_y, travel_x) in enumerate(travels):

        @pl.when(exists(-travel_y, -travel_x))
        def _():
            place = landing(travel_y, travel_x)
            pltpu.make_async_copy(place, place, rim_recv.at[index]).wait()

    tiles = breadth // 128
    side_lane = lax.broadcasted_iota(jnp.int32, (height + 2 * RIM, 128), 1)
    for image in range(2):
        for tile in range(tiles):
            full[image * (tiles + 1) + tile] = mid[image, :, tile * 128 : (tile + 1) * 128]
        full[image * (tiles + 1) + tiles] = jnp.where(
            side_lane < 64, right_side[image], left_side[image]
        )

    def fine_image(image):
        base = image * (tiles + 1)
        return jnp.concatenate(
            [full[base + tile, 8 : height + 24] for tile in range(tiles + 1)], axis=1
        )

    def coarse_image(image):
        base = image * (tiles + 1)
        span = height // 2 + RIM
        summed = jnp.concatenate(
            [
                full[base + tile, pl.ds(0, span, stride=2), :]
                + full[base + tile, pl.ds(1, span, stride=2), :]
                for tile in range(tiles + 1)
            ],
            axis=1,
        )
        return 0.25 * (summed + moved(summed, 0, 1))

    terms_into(
        coarse_image(0), coarse_image(1), 2, 2, fixed_minds, moving_minds, coarse_terms, breadth
    )

    small_lane = lax.broadcasted_iota(jnp.int32, (8, 128), 1)
    small_row = lax.broadcasted_iota(jnp.int32, (8, 128), 0)
    first_knot = tx * cells_x - 1
    valid = (
        (small_lane < REACH_X)
        & (small_lane + first_knot >= 0)
        & (small_lane + first_knot < knots)
    )

    def displace(window, rows_ref, cols_ref):
        fields = []
        for member in range(2):
            line = None
            for k in range(REACH_X):
                part = window[member][:, k : k + 1] * cols_ref[k]
                line = part if line is None else line + part
            field = None
            for r in range(REACH_Y):
                weights = jnp.concatenate([rows_ref[r]] * tiles, axis=1)
                part = weights * line[r : r + 1, :]
                field = part if field is None else field + part
            fields.append(field)
        return fields

    def gather_up(pixels, rows_ref, cols_ref):
        compact = []
        for member in range(2):
            lines = []
            for r in range(REACH_Y):
                weights = jnp.concatenate([rows_ref[r]] * tiles, axis=1)
                lines.append(jnp.sum(weights * pixels[member], axis=0, keepdims=True))
            lines.append(jnp.zeros((8 - REACH_Y, breadth), F32))
            line = jnp.concatenate(lines, axis=0)
            out = jnp.zeros((8, 128), F32)
            for k in range(REACH_X):
                column = jnp.sum(line * cols_ref[k], axis=1, keepdims=True)
                out = jnp.where(small_lane == k, column, out)
            compact.append(jnp.where(valid, out, 0.0))
        return compact

    def message(sets, width):
        out = [None] * (width // 128)
        for number, members in enumerate(sets):
            for member in range(2):
                start = (2 * number + member) * knots
                shift = lax.rem(first_knot + 128 + start % 128, 128)
                part = pltpu.roll(members[member], shift, 1)
                at = start // 128
                out[at] = part if out[at] is None else out[at] + part
        return out

    def send(turn, pieces):
        box = boxes[turn]
        for at, piece in enumerate(pieces):
            box[me, :, at * 128 : (at + 1) * 128] = piece

        def act(device):
            pltpu.make_async_remote_copy(
                src_ref=box.at[me],
                dst_ref=box.at[me],
                send_sem=send_sem.at[turn],
                recv_sem=recv_sem.at[turn],
                device_id=device,
                device_id_type=MESH,
            ).start()

        for_peers(act)

    def arrive(turn):
        part = boxes[turn].at[0 : count - 1]
        pltpu.make_async_copy(part, part, recv_sem.at[turn]).wait()

    grid_rows = grid_sum.shape[0]

    def collect(turn, set_count):
        width = widths[turn]
        wide_row = lax.broadcasted_iota(jnp.int32, (8, width), 0)
        grid_sum[:, :width] = jnp.zeros((grid_rows, width), F32)
        extra = None
        for t in range(count_y):
            tile = boxes[turn][t * count_x]
            for j in range(1, count_x):
                tile = tile + boxes[turn][t * count_x + j]
            extra = tile if extra is None else extra + tile
            if set_count:
                grid_sum[2 * t : 2 * t + 8, :width] += jnp.where(wide_row < REACH_Y, tile, 0.0)
        extra = jnp.sum(
            jnp.where(wide_row[:, :128] == 7, extra[:, :128], 0.0), keepdims=True
        )
        set_width = max(128, 2 * knots)
        grid_row = lax.broadcasted_iota(jnp.int32, (grid_rows, set_width), 0)
        grid_lane = lax.broadcasted_iota(jnp.int32, (grid_rows, set_width), 1)
        keep = (
            (grid_row >= 1) & (grid_row <= count_y * cells_y) & (grid_lane < 2 * knots)
        )
        out = []
        for number in range(set_count):
            start = number * 2 * knots
            at = start - start % 128
            part = grid_sum[:, at : at + set_width]
            if start % 128:
                part = pltpu.roll(part, set_width - start % 128, 1)
            out.append(jnp.where(keep, part, 0.0))
        return out, extra

    def window_of(grid):
        picked = jnp.zeros((8, grid.shape[1]), F32)
        for t in range(count_y):
            picked = jnp.where(ty == t, grid[2 * t : 2 * t + 8], picked)
        out = []
        for member in range(2):
            start = member * knots
            at = start - start % 128
            shift = lax.rem(128 + 128 - start % 128 - first_knot, 128)
            part = pltpu.roll(picked[:, at : at + 128], shift, 1)
            out.append(jnp.where(valid, part, 0.0))
        return out

    def dot(left, right):
        return jnp.sum(left * right, keepdims=True)

    def pulled(terms_ref, motion):
        return (
            terms_ref[2] * motion[0] + terms_ref[3] * motion[1],
            terms_ref[3] * motion[0] + terms_ref[4] * motion[1],
        )

    def weighted(weight_ref, pair):
        return [weight_ref[...] * pair[0], weight_ref[...] * pair[1]]

    def density_row(weight_ref, motion, pull):
        dense = weight_ref[...] * (motion[0] * pull[0] + motion[1] * pull[1])
        line = jnp.sum(dense, axis=0, keepdims=True)
        total = line[:, :128]
        for tile in range(1, tiles):
            total = total + line[:, tile * 128 : (tile + 1) * 128]
        return jnp.where(small_row == 7, total, 0.0)

    part = gather_up(
        weighted(coarse_weight, (coarse_terms[0], coarse_terms[1])), coarse_rows, coarse_cols
    )
    send(0, message([part], widths[0]))
    terms_into(fine_image(0), fine_image(1), 1, 1, fixed_minds, moving_minds, fine_terms, breadth)
    fine_start = gather_up(
        weighted(fine_weight, (fine_terms[0], fine_terms[1])), fine_rows, fine_cols
    )
    arrive(0)
    (direction0,), _ = collect(0, 1)
    norm0 = dot(direction0, direction0)

    window = window_of(direction0)
    motion = displace(window, coarse_rows, coarse_cols)
    part = gather_up(
        weighted(coarse_weight, pulled(coarse_terms, motion)), coarse_rows, coarse_cols
    )
    send(1, message([part, fine_start], widths[1]))
    fine_motion0 = displace(window, fine_rows, fine_cols)
    fine_part0 = gather_up(
        weighted(fine_weight, pulled(fine_terms, fine_motion0)), fine_rows, fine_cols
    )
    arrive(1)
    (image0, fine_gradient), _ = collect(1, 2)
    step0 = norm0 / dot(direction0, image0)
    direction1 = direction0 - step0 * image0
    norm1 = dot(direction1, direction1)

    window = window_of(direction1)
    motion = displace(window, coarse_rows, coarse_cols)
    dense = density_row(coarse_weight, motion, pulled(coarse_terms, motion))
    fine_motion1 = displace(window, fine_rows, fine_cols)
    fine_part1 = gather_up(
        weighted(fine_weight, pulled(fine_terms, fine_motion1)), fine_rows, fine_cols
    )
    pieces = message([fine_part0, fine_part1], widths[2])
    pieces[0] = pieces[0] + dense
    send(2, pieces)
    arrive(2)
    (image0, image1), curvature = collect(2, 2)
    step1 = norm1 / curvature
    control = -step0 * direction0 - step1 * direction1
    direction2 = fine_gradient - step0 * image0 - step1 * image1
    norm2 = dot(direction2, direction2)

    window = window_of(direction2)
    motion2 = displace(window, fine_rows, fine_cols)
    part = gather_up(
        weighted(fine_weight, pulled(fine_terms, motion2)), fine_rows, fine_cols
    )
    send(3, message([part], widths[3]))
    field_y = -step0 * fine_motion0[0] - step1 * fine_motion1[0]
    field_x = -step0 * fine_motion0[1] - step1 * fine_motion1[1]
    arrive(3)
    (image2,), _ = collect(3, 1)
    step2 = norm2 / dot(direction2, image2)
    direction3 = direction2 - step2 * image2
    norm3 = dot(direction3, direction3)

    motion3 = displace(window_of(direction3), fine_rows, fine_cols)
    pull3 = pulled(fine_terms, motion3)
    send(4, [density_row(fine_weight, motion3, pull3)])
    control = control - step2 * direction2
    control_window = window_of(control)
    direction_window = window_of(direction3)
    field_y = field_y - step2 * motion2[0]
    field_x = field_x - step2 * motion2[1]
    pull_y, pull_x = pulled(fine_terms, (field_y, field_x))
    constant = (
        fine_terms[5]
        + 2.0 * (fine_terms[0] * field_y + fine_terms[1] * field_x)
        + field_y * pull_y
        + field_x * pull_x
    )
    linear = 2.0 * (
        (fine_terms[0] + pull_y) * motion3[0] + (fine_terms[1] + pull_x) * motion3[1]
    )
    square = motion3[0] * pull3[0] + motion3[1] * pull3[1]
    arrive(4)
    _, curvature = collect(4, 0)
    step3 = norm3 / curvature
    mismatch_ref[...] = constant - step3 * (linear - step3 * square)
    for member in range(2):
        own = control_window[member] - step3 * direction_window[member]
        coef_ref[member] = own[1 : 1 + cells_y, 1 : 1 + cells_x]

    for index, (travel_y, travel_x) in enumerate(travels):

        @pl.when(exists(travel_y, travel_x))
        def _():
            place = landing(travel_y, travel_x)
            pltpu.make_async_copy(place, place, rim_send.at[index]).wait()

    for turn in range(rounds):
        part = boxes[turn].at[0 : count - 1]
        pltpu.make_async_copy(part, part, send_sem.at[turn]).wait()


def shards(count_y, count_x, fixed_image, moving_image, tissue):
    height, breadth = fixed_image.shape
    cells_y, cells_x = height // SPACE, breadth // SPACE
    knots = count_x * cells_x
    count = count_y * count_x
    widths = tuple(-(-sets * 2 * knots // 128) * 128 for sets in (1, 2, 2, 1)) + (128,)
    grid_rows = -(-(cells_y * (count_y - 1) + 8) // 8) * 8
    tall, full_lanes = height + 2 * RIM, breadth + 128
    vmem = pltpu.VMEM
    scratch = [
        vmem((2, tall, breadth), F32),
        vmem((2, tall, 128), F32),
        vmem((2, tall, 128), F32),
        vmem((2 * (breadth // 128 + 1), tall, 128), F32),
        vmem((12, height + 16, full_lanes), F32),
        vmem((12, height + 16, full_lanes), F32),
        vmem((6, height, breadth), F32),
        vmem((6, height // 2, breadth), F32),
        vmem((height, breadth), F32),
        vmem((height // 2, breadth), F32),
        vmem((REACH_Y, height, 128), F32),
        vmem((REACH_Y, height // 2, 128), F32),
        vmem((REACH_X, 8, breadth), F32),
        vmem((REACH_X, 8, breadth), F32),
        vmem((grid_rows, max(max(widths), 128)), F32),
    ]
    scratch += [vmem((count, 8, width), F32) for width in widths]
    scratch += [
        pltpu.SemaphoreType.DMA((8,)),
        pltpu.SemaphoreType.DMA((8,)),
        pltpu.SemaphoreType.DMA((len(widths),)),
        pltpu.SemaphoreType.DMA((len(widths),)),
    ]
    return pl.pallas_call(
        functools.partial(kernel, count_y, count_x, widths),
        out_shape=(
            jax.ShapeDtypeStruct((2, cells_y, cells_x), F32),
            jax.ShapeDtypeStruct((height, breadth), F32),
        ),
        in_specs=[
            pl.BlockSpec(memory_space=pltpu.SMEM),
            pl.BlockSpec(memory_space=pltpu.VMEM),
            pl.BlockSpec(memory_space=pltpu.VMEM),
        ],
        out_specs=(
            pl.BlockSpec(memory_space=pltpu.VMEM),
            pl.BlockSpec(memory_space=pltpu.VMEM),
        ),
        scratch_shapes=scratch,
        compiler_params=pltpu.CompilerParams(
            collective_id=0, has_side_effects=True, vmem_limit_bytes=52 * 1024 * 1024
        ),
    )(tissue, fixed_image, moving_image)


def solution(mesh):
    placed = (P("ty", "tx"), P("ty", "tx"), P("ty", "tx"))
    return jax.shard_map(
        functools.partial(shards, mesh.shape["ty"], mesh.shape["tx"]),
        mesh=mesh,
        in_specs=placed,
        out_specs=(P(None, "ty", "tx"), P("ty", "tx")),
        check_vma=False,
    )
```

time: 386 us -> 47.6 us (0.12)
  blocking collectives: 188 us -> 0 us
  starting transfers between devices: 128 us -> 0 us
  Pallas kernels: 0 us -> 43.1 us
  waiting for transfers between devices: 19.6 us -> 0 us
  other arithmetic: 17.5 us -> 0 us
  local copies, waits for them, and re-layouts: 19.5 us -> 3.56 us
  between operations: 6.96 us -> 0.65 us
  matrix products: 4.67 us -> 0 us
    psum x4 -> x0, blocking collectives: 188 us -> none  [run_level(): lax.psum((jnp.sum(direction * direction), jnp.sum(curvature_density(summe...]
    ppermute x44 -> x0, starting transfers between devices: 128 us -> none  [the longest x22 99.5 us: with_halo(): lax.ppermute(lax.slice_in_dim(block, block.shape[dim] - width, None, axis...]
    pallas_call x0 -> x1, Pallas kernels: none -> 43.1 us  [shards(): pl.pallas_call(functools.partial(kernel, count_y, count_x, widths), out_s...]
    ppermute x44 -> x0, waiting for transfers between devices: 19.6 us -> none  [the longest x22 19.5 us: with_halo(): lax.ppermute(lax.slice_in_dim(block, block.shape[dim] - width, None, axis...]
    another operation x4 -> x0, local copies, waits for them, and re-layouts: 17.6 us -> none  [shards(): stacked = jnp.stack([fixed_image, moving_image])]
    reduce_sum x9 -> x0, other arithmetic: 5.23 us -> none  [the longest x4 2.73 us: run_level(): jnp.sum(direction * direction)]
    dot_general x18 -> x0, matrix products: 4.67 us -> none  [sandwich(): return jnp.einsum('pa,cab,qb->cpq', left, values, right, precision=highest)]
    add x7 -> x0, other arithmetic: 4.08 us -> none  [the longest x2 2.99 us: descriptors(): variance = sum(distances) / 12.0 + 0.1]
  transfers between devices with their start and end apart: 44 -> 0, of which waited for: 20 -> 0; matrix products, arithmetic and copies ran while one was open for 1% -> 0% of each run, Pallas kernels for 0% -> 0%
where the time goes in v1:
time: 47.6 us; the launch traced here: 47.4 us
  Pallas kernels  43.1 us (91%)
  local copies, waits for them, and re-layouts  3.56 us (7%)
  between operations  0.65 us (1%)
    pallas_call x1, Pallas kernels, shards(): pl.pallas_call(functools.partial(kernel, count_y, count_x, widths), out_s...  43.1 us
    unnamed x8, local copies, waits for them, and re-layouts  3.56 us

profile of v1, /device:TPU:0, one launch (start us, length us, event | category | flops | bytes accessed | tf_op | source)
XLA Modules:
  0.0 47.4 jit_solution(3073950156769764612)
XLA Ops:
  0.6 0.0 copy-start
  0.6 0.8 %copy-done = f32[64,256]{1,0:T(8,128)S(1)} copy-done((f32[64,256]{1,0:T(8,128)S(1)}, f32[64,256]{1,0:T(8,128)}, u32[]{:S(2)}) %copy-start) | copy-done | bytes 65560
  1.5 0.0 copy-start.1
  1.5 0.8 %copy-done.1 = f32[64,256]{1,0:T(8,128)S(1)} copy-done((f32[64,256]{1,0:T(8,128)S(1)}, f32[64,256]{1,0:T(8,128)}, u32[]{:S(2)}) %copy-start.1) | copy-done | bytes 65560
  2.3 0.0 copy-start.2
  2.3 0.7 %copy-done.2 = s32[2,8]{1,0:T(2,128)S(1)} copy-done((s32[2,8]{1,0:T(2,128)S(1)}, s32[2,8]{1,0:T(2,128)}, u32[]{:S(2)}) %copy-start.2) | copy-done | bytes 88
  3.0 43.1 %shard_map.50 = (f32[2,2,8]{2,1,0:T(2,128)S(1)}, f32[64,256]{1,0:T(8,128)S(1)}) custom-call(s32[2,8]{1,0:T(2,128)S(1)} %copy-done.2, f32[64,256]{1,0:T(8,128)S(1)} %copy-done, f32[64,256]{1,0:T(8,128)S(1)} %copy-done.1), custom_call_target="tpu_custom_call" | custom-call | tf_op jit(solution)/shard_map/pallas_call | solution.py:533
  46.1 0.6 %copy.7 = f32[2,2,8]{2,1,0:T(2,128)} copy(f32[2,2,8]{2,1,0:T(2,128)S(1)} %get-tuple-element.4) | data formatting | bytes 256
  46.7 0.6 %copy.8 = f32[64,256]{1,0:T(8,128)} copy(f32[64,256]{1,0:T(8,128)S(1)} %get-tuple-element.5) | data formatting | bytes 131072
Async XLA Ops:
  0.6 0.8 %copy-start = (f32[64,256]{1,0:T(8,128)S(1)}, f32[64,256]{1,0:T(8,128)}, u32[]{:S(2)}) copy-start(f32[64,256]{1,0:T(8,128)} %fixed_ref.1) | copy-start | bytes 196612
  1.5 0.8 %copy-start.1 = (f32[64,256]{1,0:T(8,128)S(1)}, f32[64,256]{1,0:T(8,128)}, u32[]{:S(2)}) copy-start(f32[64,256]{1,0:T(8,128)} %moving_ref.1) | copy-start | bytes 196612
  2.3 0.7 %copy-start.2 = (s32[2,8]{1,0:T(2,128)S(1)}, s32[2,8]{1,0:T(2,128)}, u32[]{:S(2)}) copy-start(s32[2,8]{1,0:T(2,128)} %tissue_ref.1) | copy-start | bytes 196

commit v2 on v1

--- a/solution.py
+++ b/solution.py
@@ -11,6 +11,9 @@
 REACH_Y = 5
 REACH_X = 11
 RIM = 16
+SEGMENT = 16
+SET = 32
+OWN_SLOT = 7
 MESH = pl.DeviceIdType.MESH
 F32 = jnp.float32
 
@@ -82,10 +85,9 @@
 def kernel(
     count_y,
     count_x,
-    widths,
-    tissue_ref,
-    fixed_ref,
-    moving_ref,
+    tissue_hbm,
+    fixed_hbm,
+    moving_hbm,
     coef_ref,
     mismatch_ref,
     mid,
@@ -102,17 +104,22 @@
     coarse_rows,
     fine_cols,
     coarse_cols,
-    grid_sum,
-    *rest,
+    tissue_ref,
+    tiles_box,
+    scalar_box,
+    load_sem,
+    rim_send,
+    rim_recv,
+    tile_send,
+    tile_recv,
+    scalar_send,
+    scalar_recv,
 ):
-    rounds = len(widths)
-    boxes = rest[:rounds]
-    rim_send, rim_recv, send_sem, recv_sem = rest[rounds:]
     ty = lax.axis_index("ty")
     tx = lax.axis_index("tx")
     count = count_y * count_x
     me = ty * count_x + tx
-    height, breadth = fixed_ref.shape
+    height, breadth = fixed_hbm.shape
     knots = count_x * (breadth // SPACE)
     cells_y, cells_x = height // SPACE, breadth // SPACE
 
@@ -132,6 +139,15 @@
 
             lax.fori_loop(1, count, body, 0)
 
+    tissue_load = pltpu.make_async_copy(tissue_hbm, tissue_ref, load_sem.at[2])
+    tissue_load.start()
+    loads = []
+    for image, ref in enumerate((fixed_hbm, moving_hbm)):
+        loads.append(
+            pltpu.make_async_copy(ref, mid.at[image, RIM : RIM + height], load_sem.at[image])
+        )
+        loads[image].start()
+
     low, high = slice(0, RIM), slice(RIM + height, 2 * RIM + height)
 
     @pl.when(ty == 0)
@@ -151,6 +167,8 @@
     @pl.when(tx == count_x - 1)
     def _():
         right_side[...] = jnp.zeros(right_side.shape, F32)
+
+    tiles_box[...] = jnp.zeros(tiles_box.shape, F32)
 
     barrier = pltpu.get_barrier_semaphore()
     for_peers(
@@ -167,6 +185,7 @@
         fine_rows[r] = bspline(row / SPACE - (r - 1.0))
         coarse_rows[r] = bspline((2.0 * coarse_row + 0.5) / SPACE - (r - 1.0))
     even = lax.rem(lane, 2) == 0
+    tissue_load.wait()
     for i in range(cells_y):
         line = jnp.zeros((8, breadth), F32)
         for j in range(cells_x):
@@ -209,7 +228,7 @@
                 lanes = slice(breadth - 128, breadth)
             else:
                 lanes = slice(0, 128)
-            for image, ref in enumerate((fixed_ref, moving_ref)):
+            for image, ref in enumerate((fixed_hbm, moving_hbm)):
                 pltpu.make_async_remote_copy(
                     src_ref=ref.at[source_rows, lanes],
                     dst_ref=landing(travel_y, travel_x).at[image],
@@ -219,8 +238,8 @@
                     device_id_type=MESH,
                 ).start()
 
-    for image, ref in enumerate((fixed_ref, moving_ref)):
-        mid[image, RIM : RIM + height] = ref[...]
+    for load in loads:
+        load.wait()
 
     for index, (travel_y, travel_x) in enumerate(travels):
 
@@ -263,19 +282,21 @@
 
     small_lane = lax.broadcasted_iota(jnp.int32, (8, 128), 1)
     small_row = lax.broadcasted_iota(jnp.int32, (8, 128), 0)
-    first_knot = tx * cells_x - 1
-    valid = (
-        (small_lane < REACH_X)
-        & (small_lane + first_knot >= 0)
-        & (small_lane + first_knot < knots)
-    )
-
-    def displace(window, rows_ref, cols_ref):
+    knot = lax.rem(small_lane, SEGMENT)
+    knot_x = tx * cells_x - 1 + knot
+    knot_y = ty * cells_y - 1 + small_row
+    valid = (knot < REACH_X) & (small_row < REACH_Y) & (knot_x >= 0) & (knot_x < knots)
+    valid = valid & (knot_y >= 0) & (knot_y < count_y * cells_y)
+    own = (small_lane < SET) & (knot >= 1) & (knot <= cells_x)
+    own = own & (small_row >= 1) & (small_row <= cells_y)
+
+    def displace(window, rows_ref, cols_ref, number=0):
         fields = []
         for member in range(2):
             line = None
             for k in range(REACH_X):
-                part = window[member][:, k : k + 1] * cols_ref[k]
+                at = number * SET + member * SEGMENT + k
+                part = window[:, at : at + 1] * cols_ref[k]
                 line = part if line is None else line + part
             field = None
             for r in range(REACH_Y):
@@ -285,8 +306,8 @@
             fields.append(field)
         return fields
 
-    def gather_up(pixels, rows_ref, cols_ref):
-        compact = []
+    def gather_up(pixels, rows_ref, cols_ref, number=0):
+        out = jnp.zeros((8, 128), F32)
         for member in range(2):
             lines = []
             for r in range(REACH_Y):
@@ -294,93 +315,98 @@
                 lines.append(jnp.sum(weights * pixels[member], axis=0, keepdims=True))
             lines.append(jnp.zeros((8 - REACH_Y, breadth), F32))
             line = jnp.concatenate(lines, axis=0)
-            out = jnp.zeros((8, 128), F32)
             for k in range(REACH_X):
                 column = jnp.sum(line * cols_ref[k], axis=1, keepdims=True)
-                out = jnp.where(small_lane == k, column, out)
-            compact.append(jnp.where(valid, out, 0.0))
-        return compact
-
-    def message(sets, width):
-        out = [None] * (width // 128)
-        for number, members in enumerate(sets):
-            for member in range(2):
-                start = (2 * number + member) * knots
-                shift = lax.rem(first_knot + 128 + start % 128, 128)
-                part = pltpu.roll(members[member], shift, 1)
-                at = start // 128
-                out[at] = part if out[at] is None else out[at] + part
+                at = number * SET + member * SEGMENT + k
+                out = jnp.where(small_lane == at, column, out)
         return out
 
-    def send(turn, pieces):
-        box = boxes[turn]
-        for at, piece in enumerate(pieces):
-            box[me, :, at * 128 : (at + 1) * 128] = piece
+    def slot_of(by_y, by_x):
+        return (by_y + 2) * 3 + by_x + 1
+
+    around = [(y, x) for y in range(-2, 3) for x in range(-1, 2) if (y, x) != (0, 0)]
+
+    def send_tile(turn, tile):
+        tiles_box[turn, OWN_SLOT] = tile
+        for by_y, by_x in around:
+
+            @pl.when(exists(by_y, by_x))
+            def _():
+                slot = slot_of(-by_y, -by_x)
+                pltpu.make_async_remote_copy(
+                    src_ref=tiles_box.at[turn, OWN_SLOT],
+                    dst_ref=tiles_box.at[turn, slot],
+                    send_sem=tile_send.at[slot],
+                    recv_sem=tile_recv.at[turn, slot],
+                    device_id=(ty + by_y, tx + by_x),
+                    device_id_type=MESH,
+                ).start()
+
+    def collect_tiles(turn):
+        for by_y, by_x in around:
+
+            @pl.when(exists(by_y, by_x))
+            def _():
+                slot = slot_of(by_y, by_x)
+                place = tiles_box.at[turn, slot]
+                pltpu.make_async_copy(place, place, tile_recv.at[turn, slot]).wait()
+
+        window = None
+        for by_x in range(-1, 2):
+            total = None
+            for by_y in range(-2, 3):
+                part = tiles_box[turn, slot_of(by_y, by_x)]
+                if by_y:
+                    part = pltpu.roll(part, (2 * by_y) % 8, 0)
+                if by_y == 2:
+                    part = jnp.where(small_row >= 4, part, 0.0)
+                if by_y == -2:
+                    part = jnp.where(small_row < 1, part, 0.0)
+                total = part if total is None else total + part
+            if by_x:
+                total = pltpu.roll(total, (8 * by_x) % 128, 1)
+                reached = (knot >= 8) if by_x > 0 else (knot < REACH_X - 8)
+                total = jnp.where(reached, total, 0.0)
+            window = total if window is None else window + total
+        return jnp.where(valid, window, 0.0)
+
+    def send_scalars(turn, row):
+        scalar_box[turn, me] = row
 
         def act(device):
             pltpu.make_async_remote_copy(
-                src_ref=box.at[me],
-                dst_ref=box.at[me],
-                send_sem=send_sem.at[turn],
-                recv_sem=recv_sem.at[turn],
+                src_ref=scalar_box.at[turn, me],
+                dst_ref=scalar_box.at[turn, me],
+                send_sem=scalar_send.at[turn],
+                recv_sem=scalar_recv.at[turn],
                 device_id=device,
                 device_id_type=MESH,
             ).start()
 
         for_peers(act)
 
-    def arrive(turn):
-        part = boxes[turn].at[0 : count - 1]
-        pltpu.make_async_copy(part, part, recv_sem.at[turn]).wait()
-
-    grid_rows = grid_sum.shape[0]
-
-    def collect(turn, set_count):
-        width = widths[turn]
-        wide_row = lax.broadcasted_iota(jnp.int32, (8, width), 0)
-        grid_sum[:, :width] = jnp.zeros((grid_rows, width), F32)
-        extra = None
-        for t in range(count_y):
-            tile = boxes[turn][t * count_x]
-            for j in range(1, count_x):
-                tile = tile + boxes[turn][t * count_x + j]
-            extra = tile if extra is None else extra + tile
-            if set_count:
-                grid_sum[2 * t : 2 * t + 8, :width] += jnp.where(wide_row < REACH_Y, tile, 0.0)
-        extra = jnp.sum(
-            jnp.where(wide_row[:, :128] == 7, extra[:, :128], 0.0), keepdims=True
-        )
-        set_width = max(128, 2 * knots)
-        grid_row = lax.broadcasted_iota(jnp.int32, (grid_rows, set_width), 0)
-        grid_lane = lax.broadcasted_iota(jnp.int32, (grid_rows, set_width), 1)
-        keep = (
-            (grid_row >= 1) & (grid_row <= count_y * cells_y) & (grid_lane < 2 * knots)
-        )
-        out = []
-        for number in range(set_count):
-            start = number * 2 * knots
-            at = start - start % 128
-            part = grid_sum[:, at : at + set_width]
-            if start % 128:
-                part = pltpu.roll(part, set_width - start % 128, 1)
-            out.append(jnp.where(keep, part, 0.0))
-        return out, extra
-
-    def window_of(grid):
-        picked = jnp.zeros((8, grid.shape[1]), F32)
-        for t in range(count_y):
-            picked = jnp.where(ty == t, grid[2 * t : 2 * t + 8], picked)
-        out = []
-        for member in range(2):
-            start = member * knots
-            at = start - start % 128
-            shift = lax.rem(128 + 128 - start % 128 - first_knot, 128)
-            part = pltpu.roll(picked[:, at : at + 128], shift, 1)
-            out.append(jnp.where(valid, part, 0.0))
-        return out
-
-    def dot(left, right):
-        return jnp.sum(left * right, keepdims=True)
+    def collect_scalars(turn):
+        part = scalar_box.at[turn, 0 : count - 1]
+        pltpu.make_async_copy(part, part, scalar_recv.at[turn]).wait()
+        row = jnp.sum(scalar_box[turn], axis=0)
+        lanes = lax.broadcasted_iota(jnp.int32, (1, 128), 1)
+        return [
+            jnp.sum(
+                jnp.where((lanes >= SET * i) & (lanes < SET * (i + 1)), row, 0.0), keepdims=True
+            )
+            for i in range(4)
+        ]
+
+    def scalars(first, second, dense):
+        third = jnp.where(own, second * second, 0.0)
+        middle = jnp.where(own, first * second, 0.0)
+        lead = jnp.where(own, first * first, 0.0)
+        packed = lead + pltpu.roll(middle, SET, 1) + pltpu.roll(third, 2 * SET, 1)
+        row = jnp.sum(packed, axis=0, keepdims=True)
+        dense = dense + pltpu.roll(dense, 64, 1)
+        dense = dense + pltpu.roll(dense, 32, 1)
+        lanes = lax.broadcasted_iota(jnp.int32, (1, 128), 1)
+        return jnp.where(lanes >= 3 * SET, dense, row)
 
     def pulled(terms_ref, motion):
         return (
@@ -397,93 +423,79 @@
         total = line[:, :128]
         for tile in range(1, tiles):
             total = total + line[:, tile * 128 : (tile + 1) * 128]
-        return jnp.where(small_row == 7, total, 0.0)
-
-    part = gather_up(
-        weighted(coarse_weight, (coarse_terms[0], coarse_terms[1])), coarse_rows, coarse_cols
-    )
-    send(0, message([part], widths[0]))
+        return total
+
+    def steps_of(first, middle, third, fourth):
+        step = first / middle
+        norm = first - 2.0 * step * middle + step * step * third
+        curvature = middle - 2.0 * step * third + step * step * fourth
+        return step, norm / curvature
+
+    send_tile(
+        0,
+        gather_up(
+            weighted(coarse_weight, (coarse_terms[0], coarse_terms[1])), coarse_rows, coarse_cols
+        ),
+    )
     terms_into(fine_image(0), fine_image(1), 1, 1, fixed_minds, moving_minds, fine_terms, breadth)
     fine_start = gather_up(
-        weighted(fine_weight, (fine_terms[0], fine_terms[1])), fine_rows, fine_cols
-    )
-    arrive(0)
-    (direction0,), _ = collect(0, 1)
-    norm0 = dot(direction0, direction0)
-
-    window = window_of(direction0)
-    motion = displace(window, coarse_rows, coarse_cols)
+        weighted(fine_weight, (fine_terms[0], fine_terms[1])), fine_rows, fine_cols, 1
+    )
+    gradient0 = collect_tiles(0)
+
+    motion = displace(gradient0, coarse_rows, coarse_cols)
     part = gather_up(
         weighted(coarse_weight, pulled(coarse_terms, motion)), coarse_rows, coarse_cols
     )
-    send(1, message([part, fine_start], widths[1]))
-    fine_motion0 = displace(window, fine_rows, fine_cols)
+    send_tile(1, part + fine_start)
+    fine_motion0 = displace(gradient0, fine_rows, fine_cols)
     fine_part0 = gather_up(
         weighted(fine_weight, pulled(fine_terms, fine_motion0)), fine_rows, fine_cols
     )
-    arrive(1)
-    (image0, fine_gradient), _ = collect(1, 2)
-    step0 = norm0 / dot(direction0, image0)
-    direction1 = direction0 - step0 * image0
-    norm1 = dot(direction1, direction1)
-
-    window = window_of(direction1)
-    motion = displace(window, coarse_rows, coarse_cols)
+    gradient1 = collect_tiles(1)
+
+    motion = displace(gradient1, coarse_rows, coarse_cols)
     dense = density_row(coarse_weight, motion, pulled(coarse_terms, motion))
-    fine_motion1 = displace(window, fine_rows, fine_cols)
+    send_scalars(0, scalars(gradient0, gradient1, dense))
+    fine_motion1 = displace(gradient1, fine_rows, fine_cols)
     fine_part1 = gather_up(
-        weighted(fine_weight, pulled(fine_terms, fine_motion1)), fine_rows, fine_cols
-    )
-    pieces = message([fine_part0, fine_part1], widths[2])
-    pieces[0] = pieces[0] + dense
-    send(2, pieces)
-    arrive(2)
-    (image0, image1), curvature = collect(2, 2)
-    step1 = norm1 / curvature
-    control = -step0 * direction0 - step1 * direction1
-    direction2 = fine_gradient - step0 * image0 - step1 * image1
-    norm2 = dot(direction2, direction2)
-
-    window = window_of(direction2)
-    motion2 = displace(window, fine_rows, fine_cols)
-    part = gather_up(
-        weighted(fine_weight, pulled(fine_terms, motion2)), fine_rows, fine_cols
-    )
-    send(3, message([part], widths[3]))
-    field_y = -step0 * fine_motion0[0] - step1 * fine_motion1[0]
-    field_x = -step0 * fine_motion0[1] - step1 * fine_motion1[1]
-    arrive(3)
-    (image2,), _ = collect(3, 1)
-    step2 = norm2 / dot(direction2, image2)
-    direction3 = direction2 - step2 * image2
-    norm3 = dot(direction3, direction3)
-
-    motion3 = displace(window_of(direction3), fine_rows, fine_cols)
-    pull3 = pulled(fine_terms, motion3)
-    send(4, [density_row(fine_weight, motion3, pull3)])
-    control = control - step2 * direction2
-    control_window = window_of(control)
-    direction_window = window_of(direction3)
-    field_y = field_y - step2 * motion2[0]
-    field_x = field_x - step2 * motion2[1]
+        weighted(fine_weight, pulled(fine_terms, fine_motion1)), fine_rows, fine_cols, 1
+    )
+    send_tile(2, fine_part0 + fine_part1)
+    fine_gradient = pltpu.roll(gradient1, 128 - SET, 1)
+    images = collect_tiles(2)
+    step0, step1 = steps_of(*collect_scalars(0))
+    near, far = -(step0 + step1), step0 * step1
+    control = near * gradient0 + far * gradient1
+    direction = fine_gradient + near * images + far * pltpu.roll(images, 128 - SET, 1)
+
+    motion2 = displace(direction, fine_rows, fine_cols)
+    send_tile(
+        3,
+        gather_up(weighted(fine_weight, pulled(fine_terms, motion2)), fine_rows, fine_cols),
+    )
+    field_y = near * fine_motion0[0] + far * fine_motion1[0]
+    field_x = near * fine_motion0[1] + far * fine_motion1[1]
+    image = collect_tiles(3)
+
+    motion3 = displace(image, fine_rows, fine_cols)
+    dense = density_row(fine_weight, motion3, pulled(fine_terms, motion3))
+    send_scalars(1, scalars(direction, image, dense))
+    step0, step1 = steps_of(*collect_scalars(1))
+    near, far = -(step0 + step1), step0 * step1
+    control = control + near * direction + far * image
+    field_y = field_y + near * motion2[0] + far * motion3[0]
+    field_x = field_x + near * motion2[1] + far * motion3[1]
     pull_y, pull_x = pulled(fine_terms, (field_y, field_x))
-    constant = (
+    mismatch_ref[...] = (
         fine_terms[5]
         + 2.0 * (fine_terms[0] * field_y + fine_terms[1] * field_x)
         + field_y * pull_y
         + field_x * pull_x
     )
-    linear = 2.0 * (
-        (fine_terms[0] + pull_y) * motion3[0] + (fine_terms[1] + pull_x) * motion3[1]
-    )
-    square = motion3[0] * pull3[0] + motion3[1] * pull3[1]
-    arrive(4)
-    _, curvature = collect(4, 0)
-    step3 = norm3 / curvature
-    mismatch_ref[...] = constant - step3 * (linear - step3 * square)
     for member in range(2):
-        own = control_window[member] - step3 * direction_window[member]
-        coef_ref[member] = own[1 : 1 + cells_y, 1 : 1 + cells_x]
+        start = member * SEGMENT + 1
+        coef_ref[member] = control[1 : 1 + cells_y, start : start + cells_x]
 
     for index, (travel_y, travel_x) in enumerate(travels):
 
@@ -492,18 +504,23 @@
             place = landing(travel_y, travel_x)
             pltpu.make_async_copy(place, place, rim_send.at[index]).wait()
 
-    for turn in range(rounds):
-        part = boxes[turn].at[0 : count - 1]
-        pltpu.make_async_copy(part, part, send_sem.at[turn]).wait()
+    for by_y, by_x in around:
+
+        @pl.when(exists(by_y, by_x))
+        def _():
+            slot = slot_of(-by_y, -by_x)
+            place = tiles_box.at[:, slot]
+            pltpu.make_async_copy(place, place, tile_send.at[slot]).wait()
+
+    for turn in range(2):
+        part = scalar_box.at[turn, 0 : count - 1]
+        pltpu.make_async_copy(part, part, scalar_send.at[turn]).wait()
 
 
 def shards(count_y, count_x, fixed_image, moving_image, tissue):
     height, breadth = fixed_image.shape
     cells_y, cells_x = height // SPACE, breadth // SPACE
-    knots = count_x * cells_x
     count = count_y * count_x
-    widths = tuple(-(-sets * 2 * knots // 128) * 128 for sets in (1, 2, 2, 1)) + (128,)
-    grid_rows = -(-(cells_y * (count_y - 1) + 8) // 8) * 8
     tall, full_lanes = height + 2 * RIM, breadth + 128
     vmem = pltpu.VMEM
     scratch = [
@@ -521,25 +538,27 @@
         vmem((REACH_Y, height // 2, 128), F32),
         vmem((REACH_X, 8, breadth), F32),
         vmem((REACH_X, 8, breadth), F32),
-        vmem((grid_rows, max(max(widths), 128)), F32),
-    ]
-    scratch += [vmem((count, 8, width), F32) for width in widths]
-    scratch += [
+        pltpu.SMEM((cells_y, cells_x), jnp.int32),
+        vmem((4, 15, 8, 128), F32),
+        vmem((2, count, 1, 128), F32),
+        pltpu.SemaphoreType.DMA((3,)),
         pltpu.SemaphoreType.DMA((8,)),
         pltpu.SemaphoreType.DMA((8,)),
-        pltpu.SemaphoreType.DMA((len(widths),)),
-        pltpu.SemaphoreType.DMA((len(widths),)),
+        pltpu.SemaphoreType.DMA((15,)),
+        pltpu.SemaphoreType.DMA((4, 15)),
+        pltpu.SemaphoreType.DMA((2,)),
+        pltpu.SemaphoreType.DMA((2,)),
     ]
     return pl.pallas_call(
-        functools.partial(kernel, count_y, count_x, widths),
+        functools.partial(kernel, count_y, count_x),
         out_shape=(
             jax.ShapeDtypeStruct((2, cells_y, cells_x), F32),
             jax.ShapeDtypeStruct((height, breadth), F32),
         ),
         in_specs=[
-            pl.BlockSpec(memory_space=pltpu.SMEM),
-            pl.BlockSpec(memory_space=pltpu.VMEM),
-            pl.BlockSpec(memory_space=pltpu.VMEM),
+            pl.BlockSpec(memory_space=pltpu.HBM),
+            pl.BlockSpec(memory_space=pltpu.HBM),
+            pl.BlockSpec(memory_space=pltpu.HBM),
         ],
         out_specs=(
             pl.BlockSpec(memory_space=pltpu.VMEM),

time: 47.6 us -> 39 us (0.82)
  Pallas kernels: 43.1 us -> 34.5 us
    pallas_call x1, Pallas kernels: 43.1 us -> 34.5 us  [shards(): pl.pallas_call(functools.partial(kernel, count_y, count_x), out_shape=(ja...]
where the time goes in v2:
time: 39 us; the launch traced here: 38.8 us
  Pallas kernels  34.5 us (88%)
  local copies, waits for them, and re-layouts  3.56 us (9%)
  between operations  0.65 us (2%)
    pallas_call x1, Pallas kernels, shards(): pl.pallas_call(functools.partial(kernel, count_y, count_x), out_shape=(ja...  34.5 us
    unnamed x8, local copies, waits for them, and re-layouts  3.56 us

profile of v2, /device:TPU:0, one launch (start us, length us, event | category | flops | bytes accessed | tf_op | source)
XLA Modules:
  0.0 38.8 jit_solution(10436197304915094615)
XLA Ops:
  0.6 0.0 copy-start
  0.6 0.8 %copy-done = f32[64,256]{1,0:T(8,128)S(1)} copy-done((f32[64,256]{1,0:T(8,128)S(1)}, f32[64,256]{1,0:T(8,128)}, u32[]{:S(2)}) %copy-start) | copy-done | bytes 65560
  1.5 0.0 copy-start.1
  1.5 0.8 %copy-done.1 = f32[64,256]{1,0:T(8,128)S(1)} copy-done((f32[64,256]{1,0:T(8,128)S(1)}, f32[64,256]{1,0:T(8,128)}, u32[]{:S(2)}) %copy-start.1) | copy-done | bytes 65560
  2.3 0.0 copy-start.2
  2.3 0.7 %copy-done.2 = s32[2,8]{1,0:T(2,128)S(1)} copy-done((s32[2,8]{1,0:T(2,128)S(1)}, s32[2,8]{1,0:T(2,128)}, u32[]{:S(2)}) %copy-start.2) | copy-done | bytes 88
  3.0 34.5 %shard_map.50 = (f32[2,2,8]{2,1,0:T(2,128)S(1)}, f32[64,256]{1,0:T(8,128)S(1)}) custom-call(s32[2,8]{1,0:T(2,128)S(1)} %copy-done.2, f32[64,256]{1,0:T(8,128)S(1)} %copy-done, f32[64,256]{1,0:T(8,128)S(1)} %copy-done.1), custom_call_target="tpu_custom_call" | custom-call | tf_op jit(solution)/shard_map/pallas_call | solution.py:552
  37.5 0.6 %copy.7 = f32[2,2,8]{2,1,0:T(2,128)} copy(f32[2,2,8]{2,1,0:T(2,128)S(1)} %get-tuple-element.4) | data formatting | bytes 256
  38.1 0.6 %copy.8 = f32[64,256]{1,0:T(8,128)} copy(f32[64,256]{1,0:T(8,128)S(1)} %get-tuple-element.5) | data formatting | bytes 131072
Async XLA Ops:
  0.6 0.8 %copy-start = (f32[64,256]{1,0:T(8,128)S(1)}, f32[64,256]{1,0:T(8,128)}, u32[]{:S(2)}) copy-start(f32[64,256]{1,0:T(8,128)} %fixed_hbm.1) | copy-start | bytes 196612
  1.5 0.8 %copy-start.1 = (f32[64,256]{1,0:T(8,128)S(1)}, f32[64,256]{1,0:T(8,128)}, u32[]{:S(2)}) copy-start(f32[64,256]{1,0:T(8,128)} %moving_hbm.1) | copy-start | bytes 196612
  2.3 0.7 %copy-start.2 = (s32[2,8]{1,0:T(2,128)S(1)}, s32[2,8]{1,0:T(2,128)}, u32[]{:S(2)}) copy-start(s32[2,8]{1,0:T(2,128)} %tissue_hbm.1) | copy-start | bytes 196

commit v3 on v2

--- a/solution.py
+++ b/solution.py
@@ -171,9 +171,27 @@
     tiles_box[...] = jnp.zeros(tiles_box.shape, F32)
 
     barrier = pltpu.get_barrier_semaphore()
-    for_peers(
-        lambda device: pl.semaphore_signal(barrier, 1, device_id=device, device_id_type=MESH)
-    )
+    near = 2 <= count_y <= 8 and 2 <= count_x <= 4
+    greeted = [(y, x) for y in range(-1, 2) for x in range(-1, 2) if (y, x) != (0, 0)]
+    if count_y == 8:
+        greeted += [(1 - count_y, 0), (count_y - 1, 0)]
+
+    def here(by_y, by_x):
+        to_y, to_x = ty + by_y, tx + by_x
+        return (to_y >= 0) & (to_y < count_y) & (to_x >= 0) & (to_x < count_x)
+
+    def greet(device):
+        pl.semaphore_signal(barrier, 1, device_id=device, device_id_type=MESH)
+
+    if near:
+        for by_y, by_x in greeted:
+
+            @pl.when(here(by_y, by_x))
+            def _():
+                greet((ty + by_y, tx + by_x))
+
+    else:
+        for_peers(greet)
 
     lane = lax.broadcasted_iota(jnp.int32, (8, breadth), 1)
     for k in range(REACH_X):
@@ -200,7 +218,15 @@
             start = i * (SPACE // 2) + part * 8
             coarse_weight[start : start + 8] = half
 
-    pl.semaphore_wait(barrier, count - 1)
+    if near:
+        edge_y = jnp.where((ty == 0) | (ty == count_y - 1), 1, 0)
+        edge_x = jnp.where((tx == 0) | (tx == count_x - 1), 1, 0)
+        greeters = (3 - edge_y) * (3 - edge_x) - 1
+        if count_y == 8:
+            greeters = greeters + edge_y
+        pl.semaphore_wait(barrier, greeters)
+    else:
+        pl.semaphore_wait(barrier, count - 1)
 
     def rows_of(travel):
         if travel == 0:
@@ -566,7 +592,7 @@
         ),
         scratch_shapes=scratch,
         compiler_params=pltpu.CompilerParams(
-            collective_id=0, has_side_effects=True, vmem_limit_bytes=52 * 1024 * 1024
+            collective_id=0, has_side_effects=True, vmem_limit_bytes=63 * 1024 * 1024
         ),
     )(tissue, fixed_image, moving_image)
 

time: 39 us -> 36.9 us (0.946)
  Pallas kernels: 34.5 us -> 33.3 us
  local copies, waits for them, and re-layouts: 3.56 us -> 2.73 us
    pallas_call x1, Pallas kernels: 34.5 us -> 33.3 us  [shards(): pl.pallas_call(functools.partial(kernel, count_y, count_x), out_shape=(ja...]
    unnamed x8 -> x4, local copies, waits for them, and re-layouts: 3.56 us -> 2.73 us
where the time goes in v3:
time: 36.9 us; the launch traced here: 36.7 us
  Pallas kernels  33.3 us (90%)
  local copies, waits for them, and re-layouts  2.73 us (7%)
  between operations  0.65 us (2%)
    pallas_call x1, Pallas kernels, shards(): pl.pallas_call(functools.partial(kernel, count_y, count_x), out_shape=(ja...  33.3 us
    unnamed x4, local copies, waits for them, and re-layouts  2.73 us

profile of v3, /device:TPU:0, one launch (start us, length us, event | category | flops | bytes accessed | tf_op | source)
XLA Modules:
  0.0 36.7 jit_solution(12551659439493304230)
XLA Ops:
  0.6 33.3 %shard_map.50 = (f32[2,2,8]{2,1,0:T(2,128)}, f32[64,256]{1,0:T(8,128)}) custom-call(s32[2,8]{1,0:T(2,128)} %tissue_hbm.1, f32[64,256]{1,0:T(8,128)} %fixed_hbm.1, f32[64,256]{1,0:T(8,128)} %moving_hbm.1), custom_call_target="tpu_custom_call" | custom-call | tf_op jit(solution)/shard_map/pallas_call | solution.py:578
  33.9 0.0 copy-start
  33.9 0.7 %copy-done = f32[2,2,8]{2,1,0:T(2,128)S(1)} copy-done((f32[2,2,8]{2,1,0:T(2,128)S(1)}, f32[2,2,8]{2,1,0:T(2,128)}, u32[]{:S(2)}) %copy-start) | copy-done | bytes 152
  34.6 0.6 %copy.7 = f32[2,2,8]{2,1,0:T(2,128)} copy(f32[2,2,8]{2,1,0:T(2,128)S(1)} %copy-done) | data formatting | bytes 256
  35.2 1.5 %copy.8 = f32[64,256]{1,0:T(8,128)} copy(f32[64,256]{1,0:T(8,128)} %get-tuple-element.5) | data formatting | bytes 131072
Async XLA Ops:
  33.9 0.7 %copy-start = (f32[2,2,8]{2,1,0:T(2,128)S(1)}, f32[2,2,8]{2,1,0:T(2,128)}, u32[]{:S(2)}) copy-start(f32[2,2,8]{2,1,0:T(2,128)} %get-tuple-element.4) | copy-start | bytes 388
